TPU v7x, 256 devices: a whole 4x4x8 slice. The times are simulated.
256 devices in a mesh: replica: 32 (over y_lo, z, core), tensor: 8 (over y_hi, x).
Axes of the slice: x: 4, y: 4 (y_hi: 2, y_lo: 2; y = y_hi * 2 + y_lo), z: 8, core: 2. Of those that a mesh axis runs over, the one named last changes fastest.
Arguments:
- queries: bfloat16 [128, 2, 8192], P('replica', None, 'tensor'), parts along dimension 0, may hold values from -16 to 16
- kv_cache: bfloat16 [2, 64, 8, 4096, 128], P(None, 'replica', 'tensor'), parts along dimension 1, may hold values from -16 to 16
- fresh_kv: bfloat16 [2, 4, 64, 8, 128], P(None, None, 'replica', 'tensor'), parts along dimension 2, may hold values from -6 to 6
- lengths: int32 [64], P('replica'), parts along dimension 0, may hold values from 512 to 4096
- spare_slot: int32 [32], P('replica'), parts along dimension 0, may hold values from 0 to 32767
- out_weight: bfloat16 [8192, 4096], P('tensor'), may hold values from -1.5 to 1.5
- residual: bfloat16 [128, 2, 4096], P('replica'), parts along dimension 0, may hold values from -3 to 3
- norm_gain: bfloat16 [4096], replicated, may hold values from 0.5 to 1.5
Outputs:
- mixed: bfloat16 [128, 2, 4096], P('replica'), parts along dimension 0
- normed: bfloat16 [128, 2, 4096], P('replica'), parts along dimension 0
There are 32 independent parts, one for each index of `replica`. A program takes and returns all parts, laid end to end along the dimension named above; an argument that names none is the same for every part. Nothing has to cross between parts.
All inputs are finite; a program needn't handle non-finite values.
Results may differ from a plain program's by a relative error of at most 0.0058.
Values may be sent and summed in bfloat16 or wider, within the bound.
A program may use at most 64 MiB of HBM per device.

v0:
```python
import math

import jax
import jax.numpy as jnp
from jax import lax
from jax.sharding import PartitionSpec as P


def passed_along(block, axis, distance):
    devices = range(lax.axis_size(axis))
    route = [((i - distance) % len(devices), i) for i in devices]
    return lax.ppermute(block, axis, route)


def attend(query_block, key_block, value_block, fresh_keys, fresh_values, lengths):
    scale_factor = 1.0 / math.sqrt(query_block.shape[-1])
    cached = (
        jnp.einsum("srgah,rgch->srgac", query_block, key_block, preferred_element_type=jnp.float32)
        * scale_factor
    )
    span_total = key_block.shape[2]
    valid_mask = jnp.arange(span_total)[None, :] < lengths[:, None]
    cached = jnp.where(valid_mask[None, :, None, None, :], cached, -1e30)
    recent = (
        jnp.einsum("srgah,trgh->srgat", query_block, fresh_keys, preferred_element_type=jnp.float32)
        * scale_factor
    )
    step_count = query_block.shape[0]
    causal = jnp.arange(step_count)[None, :] <= jnp.arange(step_count)[:, None]
    recent = jnp.where(causal[:, None, None, None, :], recent, -1e30)
    highest = jnp.maximum(jnp.max(cached, -1), jnp.max(recent, -1))[..., None]
    cached_exp = jnp.exp(cached - highest)
    recent_exp = jnp.exp(recent - highest)
    totals = jnp.sum(cached_exp, -1, keepdims=True) + jnp.sum(recent_exp, -1, keepdims=True)
    cached_weights = (cached_exp / totals).astype(jnp.bfloat16)
    recent_weights = (recent_exp / totals).astype(jnp.bfloat16)
    result = jnp.einsum(
        "srgac,rgch->srgah", cached_weights, value_block, preferred_element_type=jnp.float32
    )
    result = result + jnp.einsum(
        "srgat,trgh->srgah", recent_weights, fresh_values, preferred_element_type=jnp.float32
    )
    return result.astype(jnp.bfloat16)


def finish(stream_rows, summed, norm_gain):
    stream = stream_rows.astype(jnp.float32) + summed
    spread = jnp.mean(stream * stream, -1, keepdims=True)
    normed = stream * lax.rsqrt(spread + 1e-05) * norm_gain.astype(jnp.float32)
    return (stream.astype(jnp.bfloat16), normed.astype(jnp.bfloat16))


def shards(queries, kv_cache, fresh_kv, lengths, spare_slot, out_weight, residual, norm_gain):
    members = lax.axis_size("tensor")
    levels = members.bit_length() - 1
    step_count = queries.shape[0]
    row_count = queries.shape[1]
    local_heads = kv_cache.shape[2]
    head_width = kv_cache.shape[-1]
    local_query = queries.reshape(step_count, row_count, local_heads, -1, head_width)
    spare_index = spare_slot[0] % members
    moved_query = local_query
    for level in range(levels):
        chosen = jnp.bitwise_and(jnp.right_shift(spare_index, level), 1) == 1
        arrived_query = passed_along(moved_query, "tensor", 2**level)
        moved_query = jnp.where(chosen, arrived_query, moved_query)
    attended = attend(moved_query, kv_cache[0], kv_cache[1], fresh_kv[0], fresh_kv[1], lengths)
    for level in range(levels):
        chosen = jnp.bitwise_and(jnp.right_shift(spare_index, level), 1) == 1
        arrived_output = passed_along(attended, "tensor", members - 2**level)
        attended = jnp.where(chosen, arrived_output, attended)
    flat_heads = attended.reshape(step_count * row_count, -1)
    partial_sum = jnp.dot(flat_heads, out_weight, preferred_element_type=jnp.float32)
    stream_rows = residual.reshape(step_count * row_count, -1)
    summed = lax.psum(partial_sum, "tensor")
    mixed, normed = finish(stream_rows, summed, norm_gain)
    return (mixed.reshape(step_count, row_count, -1), normed.reshape(step_count, row_count, -1))


def solution(mesh):
    return jax.shard_map(
        shards,
        mesh=mesh,
        in_specs=(
            P("replica", None, "tensor"),
            P(None, "replica", "tensor", None, None),
            P(None, None, "replica", "tensor", None),
            P("replica"),
            P("replica"),
            P("tensor", None),
            P("replica", None, None),
            P(),
        ),
        out_specs=(P("replica", None, None), P("replica", None, None)),
        check_vma=False,
    )
```

profile of v0, /device:TPU:224, one launch (start us, length us, event | category | flops | bytes accessed | tf_op | source)
XLA Modules:
  0.0 150.0 jit_solution(16401519339051563029)
XLA Ops:
  7.2 0.0 all-reduce.2.cloned.1.call-start
  7.2 0.7 reshape.145
  8.0 1.6 %collective-permute-start = (bf16[4,2,1,8,128]{4,3,0,1,2:T(8,128)(2,1)S(1)}, bf16[4,2,1,8,128]{4,3,0,1,2:T(8,128)(2,1)S(1)}, u32[]{:S(2)}, u32[]{:S(2)}) collective-permute-start(bf16[4,2,1,8,128]{4,3,0,1,2:T(8,128)(2,1)S(1)} %copy.25), channel_id=1, source_target_pairs={{7,0},{0,1},{1,2},{2,3},{3,4},{4,5},{5,6},{6,7},{15,8},{8,9},{9,10... | collective-permute-start | bytes 49160 | tf_op jit(solution)/shard_map/ppermute | solution.py:12
  9.5 0.7 iota_compare_fusion
  10.9 4.5 %collective-permute-done = bf16[4,2,1,8,128]{4,3,0,1,2:T(8,128)(2,1)S(1)} collective-permute-done((bf16[4,2,1,8,128]{4,3,0,1,2:T(8,128)(2,1)S(1)}, bf16[4,2,1,8,128]{4,3,0,1,2:T(8,128)(2,1)S(1)}, u32[]{:S(2)}, u32[]{:S(2)}) %collective-permute-start) | collective-permute-done | bytes 16416 | tf_op jit(solution)/shard_map/ppermute | solution.py:12
  15.4 0.0 collective-permute-start.1
  15.4 0.7 fusion.19
  16.1 6.9 %collective-permute-done.1 = bf16[4,2,1,8,128]{4,3,0,1,2:T(8,128)(2,1)S(1)} collective-permute-done((bf16[4,2,1,8,128]{4,3,0,1,2:T(8,128)(2,1)S(1)}, bf16[4,2,1,8,128]{4,3,0,1,2:T(8,128)(2,1)S(1)}, u32[]{:S(2)}, u32[]{:S(2)}) %collective-permute-start.1) | collective-permute-done | bytes 16416 | tf_op jit(solution)/shard_map/ppermute | solution.py:12
  23.0 3.2 %collective-permute-start.2 = (bf16[4,2,1,8,128]{4,3,0,1,2:T(8,128)(2,1)S(1)}, bf16[4,2,1,8,128]{4,3,0,1,2:T(8,128)(2,1)S(1)}, u32[]{:S(2)}, u32[]{:S(2)}) collective-permute-start(bf16[4,2,1,8,128]{4,3,0,1,2:T(8,128)(2,1)S(1)} %broadcast_select_fusion.3), channel_id=1, source_target_pairs={{4,0},{5,1},{6,2},{7,3},{0,4},{1,5},{2,6},{3,7},{12,8},{13,9},{14,... | collective-permute-start | bytes 49160 | tf_op jit(solution)/shard_map/ppermute | solution.py:12
  26.2 2.0 %collective-permute-done.2 = bf16[4,2,1,8,128]{4,3,0,1,2:T(8,128)(2,1)S(1)} collective-permute-done((bf16[4,2,1,8,128]{4,3,0,1,2:T(8,128)(2,1)S(1)}, bf16[4,2,1,8,128]{4,3,0,1,2:T(8,128)(2,1)S(1)}, u32[]{:S(2)}, u32[]{:S(2)}) %collective-permute-start.2) | collective-permute-done | bytes 16416 | tf_op jit(solution)/shard_map/ppermute | solution.py:12
  28.3 2.6 %fusion.20 = (f32[4,2,8]{2,0,1:T(4,128)S(1)}, f32[4,2,1,8,4096]{4,3,0,1,2:T(8,128)S(1)}) fusion(bf16[2,2,1,4096,128]{4,3,1,2,0:T(8,128)(2,1)} %bitcast.84, bf16[4,2,1,8,128]{4,3,0,1,2:T(8,128)(2,1)S(1)} %collective-permute-done.2, bf16[4,2,1,8,128]{4,3,0,1,2:T(8,128)(2,1)S(1)} %broadcast_select_fusion.3, pred[]{:T(512)S(6)} %eq.14, ...), kind=kOutput, calls=%fused_computation.42 | convolution fusion | flops 67903424 | bytes 3186945 | tf_op jit(solution)/shard_map/srgah,rgch->srgac/dot_general | solution.py:18
  30.9 0.2 fusion.21
  31.2 0.3 fusion.8
  31.5 2.1 %fusion.3 = f32[2,4,8,128]{3,2,1,0:T(8,128)S(1)} fusion(bf16[2,2,1,4096,128]{4,3,1,2,0:T(8,128)(2,1)} %bitcast.85, f32[4,2,1,8,4096]{4,3,0,1,2:T(8,128)S(1)} %get-tuple-element.9, f32[4,2,8]{2,0,1:T(4,128)S(1)} %add.32, f32[4,2,8]{2,0,1:T(4,128)S(1)} %max.9), kind=kOutput, calls=%fused_computation.5 | convolution fusion | flops 67895296 | bytes 3179008 | tf_op jit(solution)/shard_map/srgac,rgch->srgah/dot_general | solution.py:37
  33.6 0.2 fusion.5
  33.8 0.0 collective-permute-start.3
  33.8 3.7 %collective-permute-done.3 = bf16[4,2,1,8,128]{4,3,0,1,2:T(8,128)(2,1)S(1)} collective-permute-done((bf16[4,2,1,8,128]{4,3,0,1,2:T(8,128)(2,1)S(1)}, bf16[4,2,1,8,128]{4,3,0,1,2:T(8,128)(2,1)S(1)}, u32[]{:S(2)}, u32[]{:S(2)}) %collective-permute-start.3) | collective-permute-done | bytes 16416 | tf_op jit(solution)/shard_map/ppermute | solution.py:12
  37.5 0.3 collective-permute-start.4
  37.8 5.0 %collective-permute-done.4 = bf16[4,2,1,8,128]{4,3,0,1,2:T(8,128)(2,1)S(1)} collective-permute-done((bf16[4,2,1,8,128]{4,3,0,1,2:T(8,128)(2,1)S(1)}, bf16[4,2,1,8,128]{4,3,0,1,2:T(8,128)(2,1)S(1)}, u32[]{:S(2)}, u32[]{:S(2)}) %collective-permute-start.4) | collective-permute-done | bytes 16416 | tf_op jit(solution)/shard_map/ppermute | solution.py:12
  42.8 3.2 %collective-permute-start.5 = (bf16[4,2,1,8,128]{4,3,0,1,2:T(8,128)(2,1)S(1)}, bf16[4,2,1,8,128]{4,3,0,1,2:T(8,128)(2,1)S(1)}, u32[]{:S(2)}, u32[]{:S(2)}) collective-permute-start(bf16[4,2,1,8,128]{4,3,0,1,2:T(8,128)(2,1)S(1)} %broadcast_select_fusion.2), channel_id=1, source_target_pairs={{4,0},{5,1},{6,2},{7,3},{0,4},{1,5},{2,6},{3,7},{12,8},{13,9},{14,... | collective-permute-start | bytes 49160 | tf_op jit(solution)/shard_map/ppermute | solution.py:12
  46.0 2.0 %collective-permute-done.5 = bf16[4,2,1,8,128]{4,3,0,1,2:T(8,128)(2,1)S(1)} collective-permute-done((bf16[4,2,1,8,128]{4,3,0,1,2:T(8,128)(2,1)S(1)}, bf16[4,2,1,8,128]{4,3,0,1,2:T(8,128)(2,1)S(1)}, u32[]{:S(2)}, u32[]{:S(2)}) %collective-permute-start.5) | collective-permute-done | bytes 16416 | tf_op jit(solution)/shard_map/ppermute | solution.py:12
  48.0 0.0 copy-done
  48.0 0.0 copy-start.1
  48.0 0.0 copy-start.2
  48.1 1.9 %fusion.11 = f32[8,4096]{1,0:T(8,128)} fusion(bf16[1024,4096]{1,0:T(8,128)(2,1)S(1)} %copy-done, bf16[1,8,8,128]{3,2,1,0:T(8,128)(2,1)S(1)} %bitcast.86), kind=kOutput, calls=%fused_computation.21 | convolution fusion | flops 67108864 | bytes 8536064 | tf_op jit(solution)/shard_map/dot_general | solution.py:73
  49.9 0.0 all-reduce.2.cloned.1.call-update
  50.0 0.0 copy-done.2
  50.0 90.6 %all-reduce.2.cloned.1.call-done = f32[8,4096]{1,0:T(8,128)} async-done(((f32[8,4096]{1,0:T(8,128)}), f32[8,4096]{1,0:T(8,128)}) %all-reduce.2.cloned.1.call-update) | async-done | bytes 131088 | tf_op jit(solution)/shard_map/psum | solution.py:75
  140.6 1.1 multiply_reduce_fusion
  141.7 0.1 multiply_convert_fusion
  141.8 0.7 reshape.138
  142.4 0.7 reshape.139
  (16 shorter events, 0.1 us)
Async XLA Ops:
  7.2 133.4 %all-reduce.2.cloned.1.call-start = ((), (), s32[]{:S(2)}) async-start(), calls=%async_computation | async-start | bytes 262144 | tf_op jit(solution)/shard_map/psum | solution.py:75
  8.0 7.4 %collective-permute-start = (bf16[4,2,1,8,128]{4,3,0,1,2:T(8,128)(2,1)S(1)}, bf16[4,2,1,8,128]{4,3,0,1,2:T(8,128)(2,1)S(1)}, u32[]{:S(2)}, u32[]{:S(2)}) collective-permute-start(bf16[4,2,1,8,128]{4,3,0,1,2:T(8,128)(2,1)S(1)} %copy.25), channel_id=1, source_target_pairs={{7,0},{0,1},{1,2},{2,3},{3,4},{4,5},{5,6},{6,7},{15,8},{8,9},{9,10... | collective-permute-start | bytes 49160 | tf_op jit(solution)/shard_map/ppermute | solution.py:12
  15.4 7.6 %collective-permute-start.1 = (bf16[4,2,1,8,128]{4,3,0,1,2:T(8,128)(2,1)S(1)}, bf16[4,2,1,8,128]{4,3,0,1,2:T(8,128)(2,1)S(1)}, u32[]{:S(2)}, u32[]{:S(2)}) collective-permute-start(bf16[4,2,1,8,128]{4,3,0,1,2:T(8,128)(2,1)S(1)} %broadcast_select_fusion.1), channel_id=1, source_target_pairs={{6,0},{7,1},{0,2},{1,3},{2,4},{3,5},{4,6},{5,7},{14,8},{15,9},{8,1... | collective-permute-start | bytes 49160 | tf_op jit(solution)/shard_map/ppermute | solution.py:12
  23.0 5.2 %collective-permute-start.2 = (bf16[4,2,1,8,128]{4,3,0,1,2:T(8,128)(2,1)S(1)}, bf16[4,2,1,8,128]{4,3,0,1,2:T(8,128)(2,1)S(1)}, u32[]{:S(2)}, u32[]{:S(2)}) collective-permute-start(bf16[4,2,1,8,128]{4,3,0,1,2:T(8,128)(2,1)S(1)} %broadcast_select_fusion.3), channel_id=1, source_target_pairs={{4,0},{5,1},{6,2},{7,3},{0,4},{1,5},{2,6},{3,7},{12,8},{13,9},{14,... | collective-permute-start | bytes 49160 | tf_op jit(solution)/shard_map/ppermute | solution.py:12
  28.3 19.7 %copy-start = (bf16[1024,4096]{1,0:T(8,128)(2,1)S(1)}, bf16[1024,4096]{1,0:T(8,128)(2,1)}, u32[]{:S(2)}) copy-start(bf16[1024,4096]{1,0:T(8,128)(2,1)} %param.13) | copy-start | bytes 25165828
  33.8 3.7 %collective-permute-start.3 = (bf16[4,2,1,8,128]{4,3,0,1,2:T(8,128)(2,1)S(1)}, bf16[4,2,1,8,128]{4,3,0,1,2:T(8,128)(2,1)S(1)}, u32[]{:S(2)}, u32[]{:S(2)}) collective-permute-start(bf16[4,2,1,8,128]{4,3,0,1,2:T(8,128)(2,1)S(1)} %fusion.5), channel_id=1, source_target_pairs={{1,0},{2,1},{3,2},{4,3},{5,4},{6,5},{7,6},{0,7},{9,8},{10,9},{11,1... | collective-permute-start | bytes 49160 | tf_op jit(solution)/shard_map/ppermute | solution.py:12
  37.5 5.2 %collective-permute-start.4 = (bf16[4,2,1,8,128]{4,3,0,1,2:T(8,128)(2,1)S(1)}, bf16[4,2,1,8,128]{4,3,0,1,2:T(8,128)(2,1)S(1)}, u32[]{:S(2)}, u32[]{:S(2)}) collective-permute-start(bf16[4,2,1,8,128]{4,3,0,1,2:T(8,128)(2,1)S(1)} %broadcast_select_fusion), channel_id=1, source_target_pairs={{2,0},{3,1},{4,2},{5,3},{6,4},{7,5},{0,6},{1,7},{10,8},{11,9},{12,... | collective-permute-start | bytes 49160 | tf_op jit(solution)/shard_map/ppermute | solution.py:12
  42.8 5.2 %collective-permute-start.5 = (bf16[4,2,1,8,128]{4,3,0,1,2:T(8,128)(2,1)S(1)}, bf16[4,2,1,8,128]{4,3,0,1,2:T(8,128)(2,1)S(1)}, u32[]{:S(2)}, u32[]{:S(2)}) collective-permute-start(bf16[4,2,1,8,128]{4,3,0,1,2:T(8,128)(2,1)S(1)} %broadcast_select_fusion.2), channel_id=1, source_target_pairs={{4,0},{5,1},{6,2},{7,3},{0,4},{1,5},{2,6},{3,7},{12,8},{13,9},{14,... | collective-permute-start | bytes 49160 | tf_op jit(solution)/shard_map/ppermute | solution.py:12
  48.0 1.9 %copy-start.1 = (bf16[4,2,4096]{2,1,0:T(2,128)(2,1)S(1)}, bf16[4,2,4096]{2,1,0:T(2,128)(2,1)}, u32[]{:S(2)}) copy-start(bf16[4,2,4096]{2,1,0:T(2,128)(2,1)} %param.14) | copy-start | bytes 196612
  48.0 1.9 %copy-start.2 = (bf16[4096]{0:T(1024)(128)(2,1)S(1)}, bf16[4096]{0:T(1024)(128)(2,1)}, u32[]{:S(2)}) copy-start(bf16[4096]{0:T(1024)(128)(2,1)} %param.15) | copy-start | bytes 24580
Sparse Core Ops, SparseCore 0:
  50.1 90.4 all-reduce.1
where the time goes:
time: 152 us; the launch traced here: 150 us
  waiting for transfers between devices  115 us (76%)
  between operations  14.8 us (10%)
  starting transfers between devices  8.28 us (5%)
  matrix products  6.95 us (5%)
  local copies, waits for them, and re-layouts  2.86 us (2%)
  other arithmetic  2.29 us (2%)
    psum x1, waiting for transfers between devices, shards(): summed = lax.psum(partial_sum, 'tensor')  90.6 us
    ppermute x6, waiting for transfers between devices, passed_along(): return lax.ppermute(block, axis, route)  24.2 us
    ppermute x6, starting transfers between devices, passed_along(): return lax.ppermute(block, axis, route)  8.24 us
  transfers between devices with their start and end apart: 7, of which 7 were waited for; matrix products, arithmetic and copies ran while one was open for 1% of the time, Pallas kernels for 0%

commit v1 on v0

v1 whole, which is shorter than its diff:
```python
import functools
import math

import jax
import jax.numpy as jnp
from jax import lax
from jax.experimental import pallas as pl
from jax.experimental.pallas import tpu as pltpu
from jax.sharding import PartitionSpec as P

N = 8
PAD = 128
ORDER = (6, 5, 7, 4, 2, 1, 3)


def partner(me, offset):
    high = lax.rem(me // 4 + offset // 4, 2)
    low = lax.rem(lax.rem(me, 4) + offset % 4, 4)
    return high * 4 + low


def kernel(
    q_hbm, kv_hbm, fresh_hbm, len_hbm, spare_hbm, w_hbm, res_hbm, gain_hbm,
    mixed_out, normed_out,
    q_raw, kv, fresh_raw, len_s, spare_s, w, res_raw, gain,
    rows_f32, heads_f32, fresh_f32, q_all, o_all, sums_out, sums_in, mixed_all,
    local_sem, w_sem, send_sem, recv_sem,
):
    me = lax.axis_index("tensor")
    steps, seqs, width = q_raw.shape
    heads = width // 128
    ctx = kv_hbm.shape[2]
    cols = w.shape[1] // N

    barrier = pltpu.get_barrier_semaphore()
    for o in ORDER:
        pl.semaphore_signal(
            barrier, inc=1, device_id={"tensor": partner(me, o)},
            device_id_type=pl.DeviceIdType.MESH,
        )

    loads = [
        pltpu.make_async_copy(q_hbm, q_raw, local_sem.at[0]),
        pltpu.make_async_copy(len_hbm, len_s, local_sem.at[1]),
        pltpu.make_async_copy(spare_hbm, spare_s, local_sem.at[2]),
        pltpu.make_async_copy(fresh_hbm, fresh_raw, local_sem.at[3]),
    ]
    for part in range(2):
        for r in range(seqs):
            loads.append(
                pltpu.make_async_copy(
                    kv_hbm.at[part, r],
                    kv.at[part, r, pl.ds(0, ctx)],
                    local_sem.at[4 + 2 * part + r],
                )
            )
    loads.append(
        pltpu.make_async_copy(
            res_hbm.at[:, :, pl.ds(pl.multiple_of(me * cols, cols), cols)],
            res_raw, local_sem.at[8],
        )
    )
    loads.append(pltpu.make_async_copy(gain_hbm, gain, local_sem.at[9]))
    for copy in loads:
        copy.start()
    w_loads = []
    for piece in range(4):
        at = pl.ds(piece * w.shape[0] // 4, w.shape[0] // 4)
        copy = pltpu.make_async_copy(w_hbm.at[at], w.at[at], w_sem.at[piece])
        copy.start()
        w_loads.append(copy)

    def send(phase, src, buffer, o):
        copy = pltpu.make_async_remote_copy(
            src_ref=src, dst_ref=buffer.at[me],
            send_sem=send_sem.at[phase, o], recv_sem=recv_sem.at[phase, me],
            device_id={"tensor": partner(me, o)},
            device_id_type=pl.DeviceIdType.MESH,
        )
        copy.start()
        return copy

    def wait_arrivals(phase, buffer):
        for o in ORDER:
            source = partner(me, o)
            pltpu.make_async_remote_copy(
                src_ref=buffer.at[source], dst_ref=buffer.at[source],
                send_sem=send_sem.at[phase, o], recv_sem=recv_sem.at[phase, source],
                device_id={"tensor": source},
                device_id_type=pl.DeviceIdType.MESH,
            ).wait_recv()

    sent = []

    loads[0].wait()
    n_rows = heads * steps
    for s in range(steps):
        both = q_raw[s].astype(jnp.float32)
        for h in range(heads):
            at = (h * steps + s) * seqs
            heads_f32[at : at + seqs, :] = both[:, h * 128 : (h + 1) * 128]
    q_all[me] = jnp.concatenate(
        [heads_f32[pl.ds(r, n_rows, stride=seqs), :] for r in range(seqs)], 0
    ).astype(jnp.bfloat16)
    pl.semaphore_wait(barrier, N - 1)
    for o in ORDER:
        sent.append(send(0, q_all.at[me], q_all, o))

    loads[3].wait()
    for part in range(2):
        for t in range(steps):
            fresh_f32[part, 2 * t : 2 * t + 2, :] = fresh_raw[part, t].astype(jnp.float32)
    for part in range(2):
        for r in range(seqs):
            new = fresh_f32[part, pl.ds(r, steps, stride=seqs), :]
            tail = jnp.concatenate([new, jnp.zeros((PAD - steps, 128), jnp.float32)], 0)
            kv[part, r, ctx : ctx + PAD, :] = tail.astype(jnp.bfloat16)

    loads[1].wait()
    loads[2].wait()
    offset = jnp.bitwise_and(spare_s[0], N - 1)
    wait_arrivals(0, q_all)
    q = q_all[lax.rem(me - offset + N, N)]

    scale = math.log2(math.e) / math.sqrt(128)
    column = lax.broadcasted_iota(jnp.int32, (n_rows, ctx), 1)
    tail_column = lax.broadcasted_iota(jnp.int32, (n_rows, PAD), 1)
    tail_step = lax.rem(lax.broadcasted_iota(jnp.int32, (n_rows, PAD), 0), steps)
    for r in range(seqs):
        q_r = q[r * n_rows : (r + 1) * n_rows, :]
        loads[4 + r].wait()
        dims = (((1,), (1,)), ((), ()))
        cached = lax.dot_general(
            q_r, kv[0, r, 0:ctx, :], dims, preferred_element_type=jnp.float32
        )
        cached = jnp.where(column < len_s[r], cached, -1e30)
        recent = lax.dot_general(
            q_r, kv[0, r, ctx : ctx + PAD, :], dims, preferred_element_type=jnp.float32
        )
        recent = jnp.where(tail_column <= tail_step, recent, -1e30)
        top = jnp.maximum(
            jnp.max(cached, -1, keepdims=True), jnp.max(recent, -1, keepdims=True)
        )
        cached = jnp.exp2((cached - top) * scale)
        recent = jnp.exp2((recent - top) * scale)
        total = jnp.sum(cached, -1, keepdims=True) + jnp.sum(recent, -1, keepdims=True)
        share = 1.0 / total
        loads[6 + r].wait()
        out = jnp.dot(
            (cached * share).astype(jnp.bfloat16), kv[1, r, 0:ctx, :],
            preferred_element_type=jnp.float32,
        ) + jnp.dot(
            (recent * share).astype(jnp.bfloat16), kv[1, r, ctx : ctx + PAD, :],
            preferred_element_type=jnp.float32,
        )
        heads_f32[pl.ds(r, n_rows, stride=seqs), :] = out
    o_all[me] = heads_f32[...].astype(jnp.bfloat16)
    for o in ORDER:
        sent.append(send(1, o_all.at[me], o_all, o))
    for copy in w_loads:
        copy.wait()
    wait_arrivals(1, o_all)

    mine = o_all[lax.rem(me + offset, N)].astype(jnp.float32)
    n_out = steps * seqs
    lhs = jnp.concatenate(
        [mine[h * n_out : (h + 1) * n_out, :] for h in range(heads)], 1
    ).astype(jnp.bfloat16)

    def project(t):
        at = pl.ds(pl.multiple_of(t * cols, cols), cols)
        block = jnp.dot(lhs, w[:, at], preferred_element_type=jnp.float32)
        return jnp.concatenate([block[:, : cols // 2], block[:, cols // 2 :]], 0)

    for o in ORDER:
        sums_out[o] = project(partner(me, o)).astype(jnp.bfloat16)
        sent.append(send(2, sums_out.at[o], sums_in, o))
    stream = project(me)
    loads[8].wait()
    for s in range(steps):
        rows_f32[2 * s : 2 * s + 2, 0:cols] = res_raw[s].astype(jnp.float32)
    stream = stream + jnp.concatenate(
        [rows_f32[:, 0 : cols // 2], rows_f32[:, cols // 2 : cols]], 0
    )
    wait_arrivals(2, sums_in)
    for o in ORDER:
        stream = stream + sums_in[partner(me, o)].astype(jnp.float32)

    mixed_all[me] = stream.astype(jnp.bfloat16)
    for o in ORDER:
        sent.append(send(3, mixed_all.at[me], mixed_all, o))
    loads[9].wait()
    wait_arrivals(3, mixed_all)
    blocks = []
    for t in range(N):
        block = mixed_all[t].astype(jnp.float32)
        blocks += [block[:n_out], block[n_out:]]
    whole = jnp.concatenate(blocks, 1)
    spread = jnp.sum(whole * whole, -1, keepdims=True) * (1.0 / whole.shape[1])
    normed = whole * lax.rsqrt(spread + 1e-05) * gain[...].astype(jnp.float32)[None, :]
    for s in range(steps):
        mixed_out[s] = whole[2 * s : 2 * s + 2, :].astype(jnp.bfloat16)
        normed_out[s] = normed[2 * s : 2 * s + 2, :].astype(jnp.bfloat16)
    for copy in sent:
        copy.wait_send()


def shards(queries, kv_cache, fresh_kv, lengths, spare_slot, out_weight, residual, norm_gain):
    steps, seqs, width = queries.shape
    ctx = kv_cache.shape[3]
    features = out_weight.shape[1]
    heads = width // 128
    cols = features // N
    bf16, f32 = jnp.bfloat16, jnp.float32
    out = jax.ShapeDtypeStruct((steps, seqs, features), bf16)
    block = (2 * steps * seqs, cols // 2)
    return pl.pallas_call(
        kernel,
        out_shape=(out, out),
        in_specs=[pl.BlockSpec(memory_space=pltpu.HBM)] * 8,
        out_specs=(pl.BlockSpec(memory_space=pltpu.VMEM),) * 2,
        scratch_shapes=[
            pltpu.VMEM((steps, seqs, width), bf16),
            pltpu.VMEM((2, seqs, ctx + PAD, 128), bf16),
            pltpu.VMEM((2, steps, seqs, 128), bf16),
            pltpu.SMEM((seqs,), jnp.int32),
            pltpu.SMEM((1,), jnp.int32),
            pltpu.VMEM((width, features), bf16),
            pltpu.VMEM((steps, seqs, cols), bf16),
            pltpu.VMEM((features,), bf16),
            pltpu.VMEM((steps * seqs, cols), f32),
            pltpu.VMEM((seqs * heads * steps, 128), f32),
            pltpu.VMEM((2, steps * seqs, 128), f32),
            pltpu.VMEM((N, seqs * heads * steps, 128), bf16),
            pltpu.VMEM((N, seqs * heads * steps, 128), bf16),
            pltpu.VMEM((N,) + block, bf16),
            pltpu.VMEM((N,) + block, bf16),
            pltpu.VMEM((N,) + block, bf16),
            pltpu.SemaphoreType.DMA((10,)),
            pltpu.SemaphoreType.DMA((4,)),
            pltpu.SemaphoreType.DMA((4, N)),
            pltpu.SemaphoreType.DMA((4, N)),
        ],
        compiler_params=pltpu.CompilerParams(
            collective_id=0, has_side_effects=True, vmem_limit_bytes=56 * 2**20
        ),
    )(
        queries,
        kv_cache.reshape(2, seqs, ctx, 128),
        fresh_kv.reshape(2, steps, seqs, 128),
        lengths,
        spare_slot,
        out_weight,
        residual,
        norm_gain,
    )


def solution(mesh):
    return jax.shard_map(
        shards,
        mesh=mesh,
        in_specs=(
            P("replica", None, "tensor"),
            P(None, "replica", "tensor", None, None),
            P(None, None, "replica", "tensor", None),
            P("replica"),
            P("replica"),
            P("tensor", None),
            P("replica", None, None),
            P(),
        ),
        out_specs=(P("replica", None, None), P("replica", None, None)),
        check_vma=False,
    )
```

time: 152 us -> 33.1 us (0.22); the launches traced: 150 us -> 32.9 us
  waiting for transfers between devices: 115 us -> 0 us
  Pallas kernels: 0 us -> 28.6 us
  between operations: 14.8 us -> 1.29 us
  starting transfers between devices: 8.28 us -> 0 us
  matrix products: 6.95 us -> 0 us
  other arithmetic: 2.29 us -> 0 us
    psum x1 -> x0, waiting for transfers between devices: 90.6 us -> none  [shards(): summed = lax.psum(partial_sum, 'tensor')]
    pallas_call x0 -> x1, Pallas kernels: none -> 28.6 us  [shards(): pl.pallas_call(kernel, out_shape=(out, out), in_specs=[pl.BlockSpec(memor...]
    ppermute x6 -> x0, waiting for transfers between devices: 24.2 us -> none  [passed_along(): return lax.ppermute(block, axis, route)]
    ppermute x6 -> x0, starting transfers between devices: 8.24 us -> none  [passed_along(): return lax.ppermute(block, axis, route)]
    dot_general x5 -> x0, matrix products: 6.95 us -> none  [the longest x1 2.61 us: attend(): jnp.einsum('srgah,rgch->srgac', query_block, key_block, preferred_element...]
    unnamed x6 -> x2, local copies, waits for them, and re-layouts: 0.02 us -> 3.03 us
    reshape x4 -> x0, local copies, waits for them, and re-layouts: 2.11 us -> none  [the longest x2 0.74 us: shards(): queries.reshape(step_count, row_count, local_heads, -1, head_width)]
  transfers between devices with their start and end apart: 7 -> 0, of which waited for: 7 -> 0; matrix products, arithmetic and copies ran while one was open for 1% -> 0% of each run, Pallas kernels for 0% -> 0%
where the time goes in v1:
time: 33.1 us; the launch traced here: 32.9 us
  Pallas kernels  28.6 us (86%)
  local copies, waits for them, and re-layouts  3.03 us (9%)
  between operations  1.29 us (4%)
    pallas_call x1, Pallas kernels, shards(): pl.pallas_call(kernel, out_shape=(out, out), in_specs=[pl.BlockSpec(memor...  28.6 us
    unnamed x2, local copies, waits for them, and re-layouts  3.03 us

profile of v1, /device:TPU:224, one launch (start us, length us, event | category | flops | bytes accessed | tf_op | source)
XLA Modules:
  0.0 32.9 jit_solution(16950350009144731470)
XLA Ops:
  1.3 28.6 %shard_map.95 = (bf16[4,2,4096]{2,1,0:T(2,128)(2,1)}, bf16[4,2,4096]{2,1,0:T(2,128)(2,1)}) custom-call(bf16[4,2,1024]{2,1,0:T(2,128)(2,1)} %q_hbm.1, bf16[2,2,4096,128]{3,2,1,0:T(8,128)(2,1)} %bitcast.2, bf16[2,4,2,128]{3,2,1,0:T(2,128)(2,1)} %bitcast.3, s32[2]{0:T(128)} %len_hbm.1, s32[1]{0:T(128)S(6)} %copy.12.spare_hbm, bf16[1024,4096]{1,0:T(8,128)(2,1)} %w_hbm.1, ...), custom_call_target="tpu_custom_call" | custom-call | tf_op jit(solution)/shard_map/pallas_call | solution.py:217
  29.9 1.5 %copy.13 = bf16[4,2,4096]{2,1,0:T(2,128)(2,1)} copy(bf16[4,2,4096]{2,1,0:T(2,128)(2,1)} %get-tuple-element.4) | data formatting | bytes 131072
  31.4 1.5 %copy.14 = bf16[4,2,4096]{2,1,0:T(2,128)(2,1)} copy(bf16[4,2,4096]{2,1,0:T(2,128)(2,1)} %get-tuple-element.5) | data formatting | bytes 131072

commit v2 on v1

v2 whole, which is shorter than its diff:
```python
import functools
import math

import jax
import jax.numpy as jnp
from jax import lax
from jax.experimental import pallas as pl
from jax.experimental.pallas import tpu as pltpu
from jax.sharding import PartitionSpec as P

N = 8
PAD = 128
WIDE = 4
ORDER = (6, 5, 7, 4, 2, 1, 3)
ALONG_X = (2, 1, 3)


def partner(me, offset):
    high = lax.rem(me // 4 + offset // 4, 2)
    low = lax.rem(lax.rem(me, 4) + offset % 4, 4)
    return high * 4 + low


def kernel(
    q_hbm, kv_hbm, fresh_hbm, len_hbm, spare_hbm, w_hbm, res_hbm, gain_hbm,
    blocks_out, res_out, gain_out,
    q_raw, kv, fresh_raw, len_s, spare_s, w, res_raw, gain_raw,
    heads_f32, fresh_f32, q_all, o_all, sums_out, sums_in,
    local_sem, w_sem, send_sem, recv_sem,
):
    me = lax.axis_index("tensor")
    steps, seqs, width = q_raw.shape
    heads = width // 128
    ctx = kv_hbm.shape[2]
    cols = w.shape[1] // WIDE

    barrier = pltpu.get_barrier_semaphore()
    for o in ORDER:
        pl.semaphore_signal(
            barrier, inc=1, device_id={"tensor": partner(me, o)},
            device_id_type=pl.DeviceIdType.MESH,
        )

    loads = [
        pltpu.make_async_copy(q_hbm, q_raw, local_sem.at[0]),
        pltpu.make_async_copy(len_hbm, len_s, local_sem.at[1]),
        pltpu.make_async_copy(spare_hbm, spare_s, local_sem.at[2]),
        pltpu.make_async_copy(fresh_hbm, fresh_raw, local_sem.at[3]),
    ]
    for part in range(2):
        for r in range(seqs):
            loads.append(
                pltpu.make_async_copy(
                    kv_hbm.at[part, r],
                    kv.at[part, r, pl.ds(0, ctx)],
                    local_sem.at[4 + 2 * part + r],
                )
            )
    loads.append(pltpu.make_async_copy(res_hbm, res_raw, local_sem.at[8]))
    loads.append(pltpu.make_async_copy(gain_hbm, gain_raw, local_sem.at[9]))
    for copy in loads:
        copy.start()
    w_loads = []
    for piece in range(4):
        at = pl.ds(piece * w.shape[0] // 4, w.shape[0] // 4)
        copy = pltpu.make_async_copy(w_hbm.at[at], w.at[at], w_sem.at[piece])
        copy.start()
        w_loads.append(copy)

    def send(phase, src, dst, slot, o):
        copy = pltpu.make_async_remote_copy(
            src_ref=src, dst_ref=dst.at[slot],
            send_sem=send_sem.at[phase, o], recv_sem=recv_sem.at[phase, slot],
            device_id={"tensor": partner(me, o)},
            device_id_type=pl.DeviceIdType.MESH,
        )
        copy.start()
        return copy

    def wait_arrival(phase, dst, slot, o):
        pltpu.make_async_remote_copy(
            src_ref=dst.at[slot], dst_ref=dst.at[slot],
            send_sem=send_sem.at[phase, o], recv_sem=recv_sem.at[phase, slot],
            device_id={"tensor": partner(me, o)},
            device_id_type=pl.DeviceIdType.MESH,
        ).wait_recv()

    sent = []

    loads[0].wait()
    n_rows = heads * steps
    for s in range(steps):
        both = q_raw[s].astype(jnp.float32)
        for h in range(heads):
            at = (h * steps + s) * seqs
            heads_f32[at : at + seqs, :] = both[:, h * 128 : (h + 1) * 128]
    q_all[me] = jnp.concatenate(
        [heads_f32[pl.ds(r, n_rows, stride=seqs), :] for r in range(seqs)], 0
    ).astype(jnp.bfloat16)
    pl.semaphore_wait(barrier, N - 1)
    for o in ORDER:
        sent.append(send(0, q_all.at[me], q_all, me, o))

    loads[3].wait()
    for part in range(2):
        for t in range(steps):
            fresh_f32[part, 2 * t : 2 * t + 2, :] = fresh_raw[part, t].astype(jnp.float32)
    for part in range(2):
        for r in range(seqs):
            new = fresh_f32[part, pl.ds(r, steps, stride=seqs), :]
            tail = jnp.concatenate([new, jnp.zeros((PAD - steps, 128), jnp.float32)], 0)
            kv[part, r, ctx : ctx + PAD, :] = tail.astype(jnp.bfloat16)

    loads[8].wait()
    for s in range(steps):
        res_out[2 * s : 2 * s + 2, :] = res_raw[s].astype(jnp.float32)
    loads[9].wait()
    gain_out[...] = jnp.broadcast_to(
        gain_raw[...].astype(jnp.float32)[None, :], gain_out.shape
    )

    loads[1].wait()
    loads[2].wait()
    offset = jnp.bitwise_and(spare_s[0], N - 1)
    for o in ORDER:
        wait_arrival(0, q_all, partner(me, o), o)
    q = q_all[lax.rem(me - offset + N, N)]

    scale = math.log2(math.e) / math.sqrt(128)
    column = lax.broadcasted_iota(jnp.int32, (n_rows, ctx), 1)
    tail_column = lax.broadcasted_iota(jnp.int32, (n_rows, PAD), 1)
    tail_step = lax.rem(lax.broadcasted_iota(jnp.int32, (n_rows, PAD), 0), steps)
    for r in range(seqs):
        q_r = q[r * n_rows : (r + 1) * n_rows, :]
        loads[4 + r].wait()
        dims = (((1,), (1,)), ((), ()))
        cached = lax.dot_general(
            q_r, kv[0, r, 0:ctx, :], dims, preferred_element_type=jnp.float32
        )
        cached = jnp.where(column < len_s[r], cached, -1e30)
        recent = lax.dot_general(
            q_r, kv[0, r, ctx : ctx + PAD, :], dims, preferred_element_type=jnp.float32
        )
        recent = jnp.where(tail_column <= tail_step, recent, -1e30)
        top = jnp.maximum(
            jnp.max(cached, -1, keepdims=True), jnp.max(recent, -1, keepdims=True)
        )
        cached = jnp.exp2((cached - top) * scale)
        recent = jnp.exp2((recent - top) * scale)
        total = jnp.sum(cached, -1, keepdims=True) + jnp.sum(recent, -1, keepdims=True)
        share = 1.0 / total
        loads[6 + r].wait()
        out = jnp.dot(
            (cached * share).astype(jnp.bfloat16), kv[1, r, 0:ctx, :],
            preferred_element_type=jnp.float32,
        ) + jnp.dot(
            (recent * share).astype(jnp.bfloat16), kv[1, r, ctx : ctx + PAD, :],
            preferred_element_type=jnp.float32,
        )
        heads_f32[pl.ds(r, n_rows, stride=seqs), :] = out
    o_all[me] = heads_f32[...].astype(jnp.bfloat16)
    for o in ORDER:
        sent.append(send(1, o_all.at[me], o_all, me, o))
    for copy in w_loads:
        copy.wait()
    for o in ORDER:
        wait_arrival(1, o_all, partner(me, o), o)

    mine = o_all[lax.rem(me + offset, N)].astype(jnp.float32)
    n_out = steps * seqs
    lhs = jnp.concatenate(
        [mine[h * n_out : (h + 1) * n_out, :] for h in range(heads)], 1
    ).astype(jnp.bfloat16)

    def project(x):
        at = pl.ds(pl.multiple_of(x * cols, cols), cols)
        block = jnp.dot(lhs, w[:, at], preferred_element_type=jnp.float32)
        return jnp.concatenate([block[:, : cols // 2], block[:, cols // 2 :]], 0)

    x_me = lax.rem(me, WIDE)
    for o in ALONG_X:
        sums_out[o] = project(lax.rem(x_me + o, WIDE)).astype(jnp.bfloat16)
        sent.append(send(2, sums_out.at[o], sums_in, x_me, o))
    block = project(x_me)
    for o in ALONG_X:
        x = lax.rem(x_me + o, WIDE)
        wait_arrival(2, sums_in, x, o)
        block = block + sums_in[x].astype(jnp.float32)

    blocks_out[me] = block.astype(jnp.bfloat16)
    for o in ORDER:
        sent.append(send(3, blocks_out.at[me], blocks_out, me, o))
    for o in ORDER:
        wait_arrival(3, blocks_out, partner(me, o), o)
    for copy in sent:
        copy.wait_send()


def finish(blocks, res, gain, mixed_hbm, normed_hbm, mixed, normed, sems):
    steps, seqs, width = mixed_hbm.shape
    rows = steps * seqs
    parts = []
    for x in range(WIDE):
        both = blocks[x].astype(jnp.float32) + blocks[WIDE + x].astype(jnp.float32)
        parts += [both[:rows], both[rows:]]
    stream = jnp.concatenate(parts, 1) + res[...]
    for s in range(steps):
        mixed[s] = stream[seqs * s : seqs * (s + 1), :].astype(jnp.bfloat16)
    first = pltpu.make_async_copy(mixed, mixed_hbm, sems.at[0])
    first.start()
    spread = jnp.sum(stream * stream, -1, keepdims=True) * (1.0 / width)
    scaled = stream * lax.rsqrt(spread + 1e-05) * gain[...]
    for s in range(steps):
        normed[s] = scaled[seqs * s : seqs * (s + 1), :].astype(jnp.bfloat16)
    second = pltpu.make_async_copy(normed, normed_hbm, sems.at[1])
    second.start()
    first.wait()
    second.wait()


def pinned(array):
    if array.size == 1:
        return array
    return pltpu.with_memory_space_constraint(array, pltpu.HBM)


def shards(queries, kv_cache, fresh_kv, lengths, spare_slot, out_weight, residual, norm_gain):
    steps, seqs, width = queries.shape
    ctx = kv_cache.shape[3]
    features = out_weight.shape[1]
    heads = width // 128
    cols = features // WIDE
    bf16, f32 = jnp.bfloat16, jnp.float32
    rows = steps * seqs
    block = (2 * rows, cols // 2)
    args = [
        queries,
        kv_cache.reshape(2, seqs, ctx, 128),
        fresh_kv.reshape(2, steps, seqs, 128),
        lengths,
        spare_slot,
        out_weight,
        residual,
        norm_gain,
    ]
    blocks, res, gain = pl.pallas_call(
        kernel,
        out_shape=(
            pltpu.VMEM((N,) + block, bf16),
            pltpu.VMEM((rows, features), f32),
            pltpu.VMEM((rows, features), f32),
        ),
        in_specs=[pl.BlockSpec(memory_space=pltpu.HBM)] * 8,
        out_specs=(pl.BlockSpec(memory_space=pltpu.VMEM),) * 3,
        scratch_shapes=[
            pltpu.VMEM((steps, seqs, width), bf16),
            pltpu.VMEM((2, seqs, ctx + PAD, 128), bf16),
            pltpu.VMEM((2, steps, seqs, 128), bf16),
            pltpu.SMEM((seqs,), jnp.int32),
            pltpu.SMEM((1,), jnp.int32),
            pltpu.VMEM((width, features), bf16),
            pltpu.VMEM((steps, seqs, features), bf16),
            pltpu.VMEM((features,), bf16),
            pltpu.VMEM((heads * rows, 128), f32),
            pltpu.VMEM((2, rows, 128), f32),
            pltpu.VMEM((N, heads * rows, 128), bf16),
            pltpu.VMEM((N, heads * rows, 128), bf16),
            pltpu.VMEM((WIDE,) + block, bf16),
            pltpu.VMEM((WIDE,) + block, bf16),
            pltpu.SemaphoreType.DMA((10,)),
            pltpu.SemaphoreType.DMA((4,)),
            pltpu.SemaphoreType.DMA((4, N)),
            pltpu.SemaphoreType.DMA((4, N)),
        ],
        compiler_params=pltpu.CompilerParams(
            collective_id=0, has_side_effects=True, vmem_limit_bytes=32 * 2**20
        ),
    )(*[pinned(a) for a in args])
    out = pltpu.HBM((steps, seqs, features), bf16)
    return pl.pallas_call(
        finish,
        out_shape=(out, out),
        in_specs=[pl.BlockSpec(memory_space=pltpu.VMEM)] * 3,
        out_specs=(pl.BlockSpec(memory_space=pltpu.HBM),) * 2,
        scratch_shapes=[
            pltpu.VMEM((steps, seqs, features), bf16),
            pltpu.VMEM((steps, seqs, features), bf16),
            pltpu.SemaphoreType.DMA((2,)),
        ],
        compiler_params=pltpu.CompilerParams(vmem_limit_bytes=8 * 2**20),
    )(*[pltpu.with_memory_space_constraint(a, pltpu.VMEM) for a in (blocks, res, gain)])


def solution(mesh):
    return jax.shard_map(
        shards,
        mesh=mesh,
        in_specs=(
            P("replica", None, "tensor"),
            P(None, "replica", "tensor", None, None),
            P(None, None, "replica", "tensor", None),
            P("replica"),
            P("replica"),
            P("tensor", None),
            P("replica", None, None),
            P(),
        ),
        out_specs=(P("replica", None, None), P("replica", None, None)),
        check_vma=False,
    )
```

time: 33.1 us -> 28.7 us (0.87)
  local copies, waits for them, and re-layouts: 3.03 us -> 0 us
  Pallas kernels: 28.6 us -> 27.3 us
    unnamed x2 -> x0, local copies, waits for them, and re-layouts: 3.03 us -> none
    pallas_call x1 -> x2, Pallas kernels: 28.6 us -> 27.3 us  [the longest x1 26.5 us: shards(): pl.pallas_call(kernel, out_shape=(pltpu.VMEM((N,) + block, bf16), pltpu.V...]
where the time goes in v2:
time: 28.7 us; the launch traced here: 28.6 us
  Pallas kernels  27.3 us (95%)
  between operations  1.29 us (4%)
    pallas_call x1, Pallas kernels, shards(): pl.pallas_call(kernel, out_shape=(pltpu.VMEM((N,) + block, bf16), pltpu.V...  26.5 us
    pallas_call x1, Pallas kernels, shards(): pl.pallas_call(finish, out_shape=(out, out), in_specs=[pl.BlockSpec(memor...  0.79 us

profile of v2, /device:TPU:224, one launch (start us, length us, event | category | flops | bytes accessed | tf_op | source)
XLA Modules:
  0.0 28.6 jit_solution(14911955582063819095)
XLA Ops:
  1.3 26.5 %shard_map.95 = (bf16[8,16,512]{2,1,0:T(8,128)(2,1)S(1)}, f32[8,4096]{1,0:T(8,128)S(1)}, f32[8,4096]{1,0:T(8,128)S(1)}) custom-call(bf16[4,2,1024]{2,1,0:T(2,128)(2,1)} %q_hbm.1, bf16[2,2,4096,128]{3,2,1,0:T(8,128)(2,1)} %bitcast.2, bf16[2,4,2,128]{3,2,1,0:T(2,128)(2,1)} %bitcast.3, s32[2]{0:T(128)} %len_hbm.1, s32[1]{0:T(128)S(6)} %copy.10.spare_hbm, ...), custom_call_target="tpu_custom_call" | custom-call | tf_op jit(solution)/shard_map/pallas_call | solution.py:246
  27.8 0.8 %shard_map.96 = (bf16[4,2,4096]{2,1,0:T(2,128)(2,1)}, bf16[4,2,4096]{2,1,0:T(2,128)(2,1)}) custom-call(bf16[8,16,512]{2,1,0:T(8,128)(2,1)S(1)} %get-tuple-element.5.blocks, f32[8,4096]{1,0:T(8,128)S(1)} %get-tuple-element.6.res, f32[8,4096]{1,0:T(8,128)S(1)} %get-tuple-element.7.gain), custom_call_target="tpu_custom_call" | custom-call | tf_op jit(solution)/shard_map/pallas_call | solution.py:280

commit v3 on v2

--- a/solution.py
+++ b/solution.py
@@ -11,8 +11,8 @@
 N = 8
 PAD = 128
 WIDE = 4
+PIECES = 4
 ORDER = (6, 5, 7, 4, 2, 1, 3)
-ALONG_X = (2, 1, 3)
 
 
 def partner(me, offset):
@@ -21,18 +21,23 @@
     return high * 4 + low
 
 
+def slot_of(me, source):
+    high = lax.rem(me // WIDE + source // WIDE, 2)
+    low = lax.rem(lax.rem(me, WIDE) - lax.rem(source, WIDE) + WIDE, WIDE)
+    return high * WIDE + low
+
+
 def kernel(
     q_hbm, kv_hbm, fresh_hbm, len_hbm, spare_hbm, w_hbm, res_hbm, gain_hbm,
-    blocks_out, res_out, gain_out,
+    sums, res_out, gain_out,
     q_raw, kv, fresh_raw, len_s, spare_s, w, res_raw, gain_raw,
-    heads_f32, fresh_f32, q_all, o_all, sums_out, sums_in,
+    heads_f32, fresh_f32, q_all, o_all,
     local_sem, w_sem, send_sem, recv_sem,
 ):
     me = lax.axis_index("tensor")
     steps, seqs, width = q_raw.shape
     heads = width // 128
     ctx = kv_hbm.shape[2]
-    cols = w.shape[1] // WIDE
 
     barrier = pltpu.get_barrier_semaphore()
     for o in ORDER:
@@ -67,25 +72,26 @@
         copy.start()
         w_loads.append(copy)
 
-    def send(phase, src, dst, slot, o):
+    def send(phase, slots, o, piece=None):
+        src, dst = slots.at[0], slots.at[o]
+        if piece is not None:
+            src, dst = src.at[piece], dst.at[piece]
         copy = pltpu.make_async_remote_copy(
-            src_ref=src, dst_ref=dst.at[slot],
-            send_sem=send_sem.at[phase, o], recv_sem=recv_sem.at[phase, slot],
+            src_ref=src, dst_ref=dst,
+            send_sem=send_sem.at[phase], recv_sem=recv_sem.at[phase],
             device_id={"tensor": partner(me, o)},
             device_id_type=pl.DeviceIdType.MESH,
         )
         copy.start()
-        return copy
-
-    def wait_arrival(phase, dst, slot, o):
-        pltpu.make_async_remote_copy(
-            src_ref=dst.at[slot], dst_ref=dst.at[slot],
-            send_sem=send_sem.at[phase, o], recv_sem=recv_sem.at[phase, slot],
-            device_id={"tensor": partner(me, o)},
+
+    def whole(phase, slots):
+        others = slots.at[pl.ds(1, N - 1)]
+        return pltpu.make_async_remote_copy(
+            src_ref=others, dst_ref=others,
+            send_sem=send_sem.at[phase], recv_sem=recv_sem.at[phase],
+            device_id={"tensor": partner(me, 1)},
             device_id_type=pl.DeviceIdType.MESH,
-        ).wait_recv()
-
-    sent = []
+        )
 
     loads[0].wait()
     n_rows = heads * steps
@@ -94,12 +100,12 @@
         for h in range(heads):
             at = (h * steps + s) * seqs
             heads_f32[at : at + seqs, :] = both[:, h * 128 : (h + 1) * 128]
-    q_all[me] = jnp.concatenate(
+    q_all[0] = jnp.concatenate(
         [heads_f32[pl.ds(r, n_rows, stride=seqs), :] for r in range(seqs)], 0
     ).astype(jnp.bfloat16)
     pl.semaphore_wait(barrier, N - 1)
     for o in ORDER:
-        sent.append(send(0, q_all.at[me], q_all, me, o))
+        send(0, q_all, o)
 
     loads[3].wait()
     for part in range(2):
@@ -122,9 +128,8 @@
     loads[1].wait()
     loads[2].wait()
     offset = jnp.bitwise_and(spare_s[0], N - 1)
-    for o in ORDER:
-        wait_arrival(0, q_all, partner(me, o), o)
-    q = q_all[lax.rem(me - offset + N, N)]
+    whole(0, q_all).wait_recv()
+    q = q_all[slot_of(me, lax.rem(me - offset + N, N))]
 
     scale = math.log2(math.e) / math.sqrt(128)
     column = lax.broadcasted_iota(jnp.int32, (n_rows, ctx), 1)
@@ -158,51 +163,42 @@
             preferred_element_type=jnp.float32,
         )
         heads_f32[pl.ds(r, n_rows, stride=seqs), :] = out
-    o_all[me] = heads_f32[...].astype(jnp.bfloat16)
+    o_all[0] = heads_f32[...].astype(jnp.bfloat16)
     for o in ORDER:
-        sent.append(send(1, o_all.at[me], o_all, me, o))
+        send(1, o_all, o)
     for copy in w_loads:
         copy.wait()
-    for o in ORDER:
-        wait_arrival(1, o_all, partner(me, o), o)
-
-    mine = o_all[lax.rem(me + offset, N)].astype(jnp.float32)
+    whole(1, o_all).wait_recv()
+
+    mine = o_all[slot_of(me, lax.rem(me + offset, N))].astype(jnp.float32)
     n_out = steps * seqs
     lhs = jnp.concatenate(
         [mine[h * n_out : (h + 1) * n_out, :] for h in range(heads)], 1
     ).astype(jnp.bfloat16)
 
-    def project(x):
-        at = pl.ds(pl.multiple_of(x * cols, cols), cols)
+    cols = w.shape[1] // PIECES
+    for piece in range(PIECES):
+        at = pl.ds(piece * cols, cols)
         block = jnp.dot(lhs, w[:, at], preferred_element_type=jnp.float32)
-        return jnp.concatenate([block[:, : cols // 2], block[:, cols // 2 :]], 0)
-
-    x_me = lax.rem(me, WIDE)
-    for o in ALONG_X:
-        sums_out[o] = project(lax.rem(x_me + o, WIDE)).astype(jnp.bfloat16)
-        sent.append(send(2, sums_out.at[o], sums_in, x_me, o))
-    block = project(x_me)
-    for o in ALONG_X:
-        x = lax.rem(x_me + o, WIDE)
-        wait_arrival(2, sums_in, x, o)
-        block = block + sums_in[x].astype(jnp.float32)
-
-    blocks_out[me] = block.astype(jnp.bfloat16)
-    for o in ORDER:
-        sent.append(send(3, blocks_out.at[me], blocks_out, me, o))
-    for o in ORDER:
-        wait_arrival(3, blocks_out, partner(me, o), o)
-    for copy in sent:
-        copy.wait_send()
-
-
-def finish(blocks, res, gain, mixed_hbm, normed_hbm, mixed, normed, sems):
+        sums[0, piece] = jnp.concatenate(
+            [block[:, : cols // 2], block[:, cols // 2 :]], 0
+        ).astype(jnp.bfloat16)
+        for o in ORDER:
+            send(2, sums, o, piece)
+    whole(2, sums).wait_recv()
+    for phase, slots in enumerate((q_all, o_all, sums)):
+        whole(phase, slots).wait_send()
+
+
+def finish(sums, res, gain, mixed_hbm, normed_hbm, mixed, normed, sems):
     steps, seqs, width = mixed_hbm.shape
     rows = steps * seqs
     parts = []
-    for x in range(WIDE):
-        both = blocks[x].astype(jnp.float32) + blocks[WIDE + x].astype(jnp.float32)
-        parts += [both[:rows], both[rows:]]
+    for piece in range(PIECES):
+        total = sums[0, piece].astype(jnp.float32)
+        for slot in range(1, N):
+            total = total + sums[slot, piece].astype(jnp.float32)
+        parts += [total[:rows], total[rows:]]
     stream = jnp.concatenate(parts, 1) + res[...]
     for s in range(steps):
         mixed[s] = stream[seqs * s : seqs * (s + 1), :].astype(jnp.bfloat16)
@@ -229,7 +225,7 @@
     ctx = kv_cache.shape[3]
     features = out_weight.shape[1]
     heads = width // 128
-    cols = features // WIDE
+    cols = features // PIECES
     bf16, f32 = jnp.bfloat16, jnp.float32
     rows = steps * seqs
     block = (2 * rows, cols // 2)
@@ -243,10 +239,10 @@
         residual,
         norm_gain,
     ]
-    blocks, res, gain = pl.pallas_call(
+    sums, res, gain = pl.pallas_call(
         kernel,
         out_shape=(
-            pltpu.VMEM((N,) + block, bf16),
+            pltpu.VMEM((N, PIECES) + block, bf16),
             pltpu.VMEM((rows, features), f32),
             pltpu.VMEM((rows, features), f32),
         ),
@@ -265,12 +261,10 @@
             pltpu.VMEM((2, rows, 128), f32),
             pltpu.VMEM((N, heads * rows, 128), bf16),
             pltpu.VMEM((N, heads * rows, 128), bf16),
-            pltpu.VMEM((WIDE,) + block, bf16),
-            pltpu.VMEM((WIDE,) + block, bf16),
             pltpu.SemaphoreType.DMA((10,)),
             pltpu.SemaphoreType.DMA((4,)),
-            pltpu.SemaphoreType.DMA((4, N)),
-            pltpu.SemaphoreType.DMA((4, N)),
+            pltpu.SemaphoreType.DMA((3,)),
+            pltpu.SemaphoreType.DMA((3,)),
         ],
         compiler_params=pltpu.CompilerParams(
             collective_id=0, has_side_effects=True, vmem_limit_bytes=32 * 2**20
@@ -288,7 +282,7 @@
             pltpu.SemaphoreType.DMA((2,)),
         ],
         compiler_params=pltpu.CompilerParams(vmem_limit_bytes=8 * 2**20),
-    )(*[pltpu.with_memory_space_constraint(a, pltpu.VMEM) for a in (blocks, res, gain)])
+    )(*[pltpu.with_memory_space_constraint(a, pltpu.VMEM) for a in (sums, res, gain)])
 
 
 def solution(mesh):

time: 28.7 us -> 26 us (0.906)
  Pallas kernels: 27.3 us -> 24.6 us
    pallas_call x1, Pallas kernels: 26.5 us -> 23.8 us  [shards(): pl.pallas_call(kernel, out_shape=(pltpu.VMEM((N, PIECES) + block, bf16),...]
where the time goes in v3:
time: 26 us; the launch traced here: 25.9 us
  Pallas kernels  24.6 us (95%)
  between operations  1.29 us (5%)
    pallas_call x1, Pallas kernels, shards(): pl.pallas_call(kernel, out_shape=(pltpu.VMEM((N, PIECES) + block, bf16),...  23.8 us
    pallas_call x1, Pallas kernels, shards(): pl.pallas_call(finish, out_shape=(out, out), in_specs=[pl.BlockSpec(memor...  0.83 us

profile of v3, /device:TPU:224, one launch (start us, length us, event | category | flops | bytes accessed | tf_op | source)
XLA Modules:
  0.0 25.9 jit_solution(16012823963146344243)
XLA Ops:
  1.3 23.8 %shard_map.95 = (bf16[8,4,16,512]{3,2,1,0:T(8,128)(2,1)S(1)}, f32[8,4096]{1,0:T(8,128)S(1)}, f32[8,4096]{1,0:T(8,128)S(1)}) custom-call(bf16[4,2,1024]{2,1,0:T(2,128)(2,1)} %q_hbm.1, bf16[2,2,4096,128]{3,2,1,0:T(8,128)(2,1)} %bitcast.2, bf16[2,4,2,128]{3,2,1,0:T(2,128)(2,1)} %bitcast.3, s32[2]{0:T(128)} %len_hbm.1, s32[1]{0:T(128)S(6)} %copy.10.spare_hbm, ...), custom_call_target="tpu_custom_call" | custom-call | tf_op jit(solution)/shard_map/pallas_call | solution.py:242
  25.0 0.8 %shard_map.96 = (bf16[4,2,4096]{2,1,0:T(2,128)(2,1)}, bf16[4,2,4096]{2,1,0:T(2,128)(2,1)}) custom-call(bf16[8,4,16,512]{3,2,1,0:T(8,128)(2,1)S(1)} %get-tuple-element.5.sums, f32[8,4096]{1,0:T(8,128)S(1)} %get-tuple-element.6.res, f32[8,4096]{1,0:T(8,128)S(1)} %get-tuple-element.7.gain), custom_call_target="tpu_custom_call" | custom-call | tf_op jit(solution)/shard_map/pallas_call | solution.py:274

commit v4 on v3

--- a/solution.py
+++ b/solution.py
@@ -30,7 +30,7 @@
 def kernel(
     q_hbm, kv_hbm, fresh_hbm, len_hbm, spare_hbm, w_hbm, res_hbm, gain_hbm,
     sums, res_out, gain_out,
-    q_raw, kv, fresh_raw, len_s, spare_s, w, res_raw, gain_raw,
+    q_raw, keys, values, k_turned, fresh_raw, len_s, spare_s, w, res_raw, gain_raw,
     heads_f32, fresh_f32, q_all, o_all,
     local_sem, w_sem, send_sem, recv_sem,
 ):
@@ -57,7 +57,7 @@
             loads.append(
                 pltpu.make_async_copy(
                     kv_hbm.at[part, r],
-                    kv.at[part, r, pl.ds(0, ctx)],
+                    (keys, values)[part].at[pl.ds(0, ctx), pl.ds(r * 128, 128)],
                     local_sem.at[4 + 2 * part + r],
                 )
             )
@@ -115,7 +115,14 @@
         for r in range(seqs):
             new = fresh_f32[part, pl.ds(r, steps, stride=seqs), :]
             tail = jnp.concatenate([new, jnp.zeros((PAD - steps, 128), jnp.float32)], 0)
-            kv[part, r, ctx : ctx + PAD, :] = tail.astype(jnp.bfloat16)
+            (keys, values)[part][ctx : ctx + PAD, r * 128 : (r + 1) * 128] = tail.astype(
+                jnp.bfloat16
+            )
+
+    for r in range(seqs):
+        loads[4 + r].wait()
+    for low in range(0, ctx + PAD, 128):
+        k_turned[:, low : low + 128] = keys[low : low + 128, :].T
 
     loads[8].wait()
     for s in range(steps):
@@ -132,37 +139,53 @@
     q = q_all[slot_of(me, lax.rem(me - offset + N, N))]
 
     scale = math.log2(math.e) / math.sqrt(128)
-    column = lax.broadcasted_iota(jnp.int32, (n_rows, ctx), 1)
-    tail_column = lax.broadcasted_iota(jnp.int32, (n_rows, PAD), 1)
-    tail_step = lax.rem(lax.broadcasted_iota(jnp.int32, (n_rows, PAD), 0), steps)
+    none = jnp.zeros((n_rows, 128), q.dtype)
+    diagonal = jnp.concatenate(
+        [
+            jnp.concatenate([q[:n_rows], none], 1),
+            jnp.concatenate([none, q[n_rows:]], 1),
+        ],
+        0,
+    )
+    row = lax.broadcasted_iota(jnp.int32, (seqs * n_rows, 1), 0)
+    limit = jnp.where(row < n_rows, len_s[0], len_s[1])
+    step = lax.rem(row, steps)
+    top = total = out = None
+    half = ctx // 2 + PAD
+    for low, high in ((0, half), (half, ctx + PAD)):
+        scores = jnp.dot(
+            diagonal, k_turned[:, low:high], preferred_element_type=jnp.float32
+        )
+        end = min(high, ctx) - low
+        column = lax.broadcasted_iota(jnp.int32, (seqs * n_rows, end), 1)
+        masked = jnp.where(column < limit - low, scores[:, :end], -1e30)
+        if high > ctx:
+            column = lax.broadcasted_iota(jnp.int32, (seqs * n_rows, PAD), 1)
+            recent = jnp.where(column <= step, scores[:, end:], -1e30)
+            masked = jnp.concatenate([masked, recent], 1)
+        highest = jnp.max(masked, -1, keepdims=True)
+        if low > 0:
+            highest = jnp.maximum(top, highest)
+        weights = jnp.exp2((masked - highest) * scale)
+        part_total = jnp.sum(weights, -1, keepdims=True)
+        if low == 0:
+            for r in range(seqs):
+                loads[6 + r].wait()
+        part_out = jnp.dot(
+            weights.astype(jnp.bfloat16), values[low:high, :],
+            preferred_element_type=jnp.float32,
+        )
+        if low > 0:
+            shrink = jnp.exp2((top - highest) * scale)
+            part_total = part_total + total * shrink
+            part_out = part_out + out * shrink
+        top, total, out = highest, part_total, part_out
+    share = 1.0 / total
     for r in range(seqs):
-        q_r = q[r * n_rows : (r + 1) * n_rows, :]
-        loads[4 + r].wait()
-        dims = (((1,), (1,)), ((), ()))
-        cached = lax.dot_general(
-            q_r, kv[0, r, 0:ctx, :], dims, preferred_element_type=jnp.float32
-        )
-        cached = jnp.where(column < len_s[r], cached, -1e30)
-        recent = lax.dot_general(
-            q_r, kv[0, r, ctx : ctx + PAD, :], dims, preferred_element_type=jnp.float32
-        )
-        recent = jnp.where(tail_column <= tail_step, recent, -1e30)
-        top = jnp.maximum(
-            jnp.max(cached, -1, keepdims=True), jnp.max(recent, -1, keepdims=True)
-        )
-        cached = jnp.exp2((cached - top) * scale)
-        recent = jnp.exp2((recent - top) * scale)
-        total = jnp.sum(cached, -1, keepdims=True) + jnp.sum(recent, -1, keepdims=True)
-        share = 1.0 / total
-        loads[6 + r].wait()
-        out = jnp.dot(
-            (cached * share).astype(jnp.bfloat16), kv[1, r, 0:ctx, :],
-            preferred_element_type=jnp.float32,
-        ) + jnp.dot(
-            (recent * share).astype(jnp.bfloat16), kv[1, r, ctx : ctx + PAD, :],
-            preferred_element_type=jnp.float32,
-        )
-        heads_f32[pl.ds(r, n_rows, stride=seqs), :] = out
+        mine = slice(r * n_rows, (r + 1) * n_rows)
+        heads_f32[pl.ds(r, n_rows, stride=seqs), :] = (
+            out[mine, r * 128 : (r + 1) * 128] * share[mine]
+        )
     o_all[0] = heads_f32[...].astype(jnp.bfloat16)
     for o in ORDER:
         send(1, o_all, o)
@@ -250,7 +273,9 @@
         out_specs=(pl.BlockSpec(memory_space=pltpu.VMEM),) * 3,
         scratch_shapes=[
             pltpu.VMEM((steps, seqs, width), bf16),
-            pltpu.VMEM((2, seqs, ctx + PAD, 128), bf16),
+            pltpu.VMEM((ctx + PAD, seqs * 128), bf16),
+            pltpu.VMEM((ctx + PAD, seqs * 128), bf16),
+            pltpu.VMEM((seqs * 128, ctx + PAD), bf16),
             pltpu.VMEM((2, steps, seqs, 128), bf16),
             pltpu.SMEM((seqs,), jnp.int32),
             pltpu.SMEM((1,), jnp.int32),

time: 26 us -> 25.6 us (0.985)
  Pallas kernels: 24.6 us -> 24.1 us
    pallas_call x1, Pallas kernels: 23.8 us -> 23.3 us  [shards(): pl.pallas_call(kernel, out_shape=(pltpu.VMEM((N, PIECES) + block, bf16),...]
where the time goes in v4:
time: 25.6 us; the launch traced here: 25.4 us
  Pallas kernels  24.1 us (94%)
  between operations  1.29 us (5%)
    pallas_call x1, Pallas kernels, shards(): pl.pallas_call(kernel, out_shape=(pltpu.VMEM((N, PIECES) + block, bf16),...  23.3 us
    pallas_call x1, Pallas kernels, shards(): pl.pallas_call(finish, out_shape=(out, out), in_specs=[pl.BlockSpec(memor...  0.83 us

profile of v4, /device:TPU:224, one launch (start us, length us, event | category | flops | bytes accessed | tf_op | source)
XLA Modules:
  0.0 25.4 jit_solution(3039732120099733615)
XLA Ops:
  1.3 23.3 %shard_map.95 = (bf16[8,4,16,512]{3,2,1,0:T(8,128)(2,1)S(1)}, f32[8,4096]{1,0:T(8,128)S(1)}, f32[8,4096]{1,0:T(8,128)S(1)}) custom-call(bf16[4,2,1024]{2,1,0:T(2,128)(2,1)} %q_hbm.1, bf16[2,2,4096,128]{3,2,1,0:T(8,128)(2,1)} %bitcast.2, bf16[2,4,2,128]{3,2,1,0:T(2,128)(2,1)} %bitcast.3, s32[2]{0:T(128)} %len_hbm.1, s32[1]{0:T(128)S(6)} %copy.10.spare_hbm, ...), custom_call_target="tpu_custom_call" | custom-call | tf_op jit(solution)/shard_map/pallas_call | solution.py:265
  24.6 0.8 %shard_map.96 = (bf16[4,2,4096]{2,1,0:T(2,128)(2,1)}, bf16[4,2,4096]{2,1,0:T(2,128)(2,1)}) custom-call(bf16[8,4,16,512]{3,2,1,0:T(8,128)(2,1)S(1)} %get-tuple-element.5.sums, f32[8,4096]{1,0:T(8,128)S(1)} %get-tuple-element.6.res, f32[8,4096]{1,0:T(8,128)S(1)} %get-tuple-element.7.gain), custom_call_target="tpu_custom_call" | custom-call | tf_op jit(solution)/shard_map/pallas_call | solution.py:299

commit v5 on v3

--- a/solution.py
+++ b/solution.py
@@ -30,8 +30,8 @@
 def kernel(
     q_hbm, kv_hbm, fresh_hbm, len_hbm, spare_hbm, w_hbm, res_hbm, gain_hbm,
     sums, res_out, gain_out,
-    q_raw, kv, fresh_raw, len_s, spare_s, w, res_raw, gain_raw,
-    heads_f32, fresh_f32, q_all, o_all,
+    q_raw, keys, values, k_turned, fresh_raw, len_s, spare_s, w, res_raw, gain_raw,
+    heads_f32, fresh_f32, q_now, q_all, o_all,
     local_sem, w_sem, send_sem, recv_sem,
 ):
     me = lax.axis_index("tensor")
@@ -57,7 +57,7 @@
             loads.append(
                 pltpu.make_async_copy(
                     kv_hbm.at[part, r],
-                    kv.at[part, r, pl.ds(0, ctx)],
+                    (keys, values)[part].at[pl.ds(0, ctx), pl.ds(r * 128, 128)],
                     local_sem.at[4 + 2 * part + r],
                 )
             )
@@ -115,7 +115,14 @@
         for r in range(seqs):
             new = fresh_f32[part, pl.ds(r, steps, stride=seqs), :]
             tail = jnp.concatenate([new, jnp.zeros((PAD - steps, 128), jnp.float32)], 0)
-            kv[part, r, ctx : ctx + PAD, :] = tail.astype(jnp.bfloat16)
+            (keys, values)[part][ctx : ctx + PAD, r * 128 : (r + 1) * 128] = tail.astype(
+                jnp.bfloat16
+            )
+
+    for r in range(seqs):
+        loads[4 + r].wait()
+    for low in range(0, ctx + PAD, 128):
+        k_turned[:, low : low + 128] = keys[low : low + 128, :].T
 
     loads[8].wait()
     for s in range(steps):
@@ -125,66 +132,103 @@
         gain_raw[...].astype(jnp.float32)[None, :], gain_out.shape
     )
 
+    for r in range(seqs):
+        loads[6 + r].wait()
     loads[1].wait()
     loads[2].wait()
     offset = jnp.bitwise_and(spare_s[0], N - 1)
-    whole(0, q_all).wait_recv()
-    q = q_all[slot_of(me, lax.rem(me - offset + N, N))]
-
-    scale = math.log2(math.e) / math.sqrt(128)
-    column = lax.broadcasted_iota(jnp.int32, (n_rows, ctx), 1)
-    tail_column = lax.broadcasted_iota(jnp.int32, (n_rows, PAD), 1)
-    tail_step = lax.rem(lax.broadcasted_iota(jnp.int32, (n_rows, PAD), 0), steps)
-    for r in range(seqs):
-        q_r = q[r * n_rows : (r + 1) * n_rows, :]
-        loads[4 + r].wait()
-        dims = (((1,), (1,)), ((), ()))
-        cached = lax.dot_general(
-            q_r, kv[0, r, 0:ctx, :], dims, preferred_element_type=jnp.float32
+    q_now[...] = q_all[0]
+
+    def attention(turn, _):
+        @pl.when(turn == 1)
+        def _():
+            whole(0, q_all).wait_recv()
+            q_now[...] = q_all[slot_of(me, lax.rem(me - offset + N, N))]
+
+        q = q_now[...]
+
+        scale = math.log2(math.e) / math.sqrt(128)
+        none = jnp.zeros((n_rows, 128), q.dtype)
+        diagonal = jnp.concatenate(
+            [
+                jnp.concatenate([q[:n_rows], none], 1),
+                jnp.concatenate([none, q[n_rows:]], 1),
+            ],
+            0,
         )
-        cached = jnp.where(column < len_s[r], cached, -1e30)
-        recent = lax.dot_general(
-            q_r, kv[0, r, ctx : ctx + PAD, :], dims, preferred_element_type=jnp.float32
-        )
-        recent = jnp.where(tail_column <= tail_step, recent, -1e30)
-        top = jnp.maximum(
-            jnp.max(cached, -1, keepdims=True), jnp.max(recent, -1, keepdims=True)
-        )
-        cached = jnp.exp2((cached - top) * scale)
-        recent = jnp.exp2((recent - top) * scale)
-        total = jnp.sum(cached, -1, keepdims=True) + jnp.sum(recent, -1, keepdims=True)
+        row = lax.broadcasted_iota(jnp.int32, (seqs * n_rows, 1), 0)
+        limit = jnp.where(row < n_rows, len_s[0], len_s[1])
+        step = lax.rem(row, steps)
+        top = total = out = None
+        half = ctx // 2 + PAD
+        for low, high in ((0, half), (half, ctx + PAD)):
+            scores = jnp.dot(
+                diagonal, k_turned[:, low:high], preferred_element_type=jnp.float32
+            )
+            end = min(high, ctx) - low
+            column = lax.broadcasted_iota(jnp.int32, (seqs * n_rows, end), 1)
+            masked = jnp.where(column < limit - low, scores[:, :end], -1e30)
+            if high > ctx:
+                column = lax.broadcasted_iota(jnp.int32, (seqs * n_rows, PAD), 1)
+                recent = jnp.where(column <= step, scores[:, end:], -1e30)
+                masked = jnp.concatenate([masked, recent], 1)
+            highest = jnp.max(masked, -1, keepdims=True)
+            if low > 0:
+                highest = jnp.maximum(top, highest)
+            weights = jnp.exp2((masked - highest) * scale)
+            part_total = jnp.sum(weights, -1, keepdims=True)
+            part_out = jnp.dot(
+                weights.astype(jnp.bfloat16), values[low:high, :],
+                preferred_element_type=jnp.float32,
+            )
+            if low > 0:
+                shrink = jnp.exp2((top - highest) * scale)
+                part_total = part_total + total * shrink
+                part_out = part_out + out * shrink
+            top, total, out = highest, part_total, part_out
         share = 1.0 / total
-        loads[6 + r].wait()
-        out = jnp.dot(
-            (cached * share).astype(jnp.bfloat16), kv[1, r, 0:ctx, :],
-            preferred_element_type=jnp.float32,
-        ) + jnp.dot(
-            (recent * share).astype(jnp.bfloat16), kv[1, r, ctx : ctx + PAD, :],
-            preferred_element_type=jnp.float32,
-        )
-        heads_f32[pl.ds(r, n_rows, stride=seqs), :] = out
-    o_all[0] = heads_f32[...].astype(jnp.bfloat16)
+        for r in range(seqs):
+            mine = slice(r * n_rows, (r + 1) * n_rows)
+            heads_f32[pl.ds(r, n_rows, stride=seqs), :] = (
+                out[mine, r * 128 : (r + 1) * 128] * share[mine]
+            )
+        o_all[0] = heads_f32[...].astype(jnp.bfloat16)
+
+        return 0
+
+    lax.fori_loop(0, 2, attention, 0)
     for o in ORDER:
         send(1, o_all, o)
     for copy in w_loads:
         copy.wait()
-    whole(1, o_all).wait_recv()
-
-    mine = o_all[slot_of(me, lax.rem(me + offset, N))].astype(jnp.float32)
-    n_out = steps * seqs
-    lhs = jnp.concatenate(
-        [mine[h * n_out : (h + 1) * n_out, :] for h in range(heads)], 1
-    ).astype(jnp.bfloat16)
-
-    cols = w.shape[1] // PIECES
-    for piece in range(PIECES):
-        at = pl.ds(piece * cols, cols)
-        block = jnp.dot(lhs, w[:, at], preferred_element_type=jnp.float32)
-        sums[0, piece] = jnp.concatenate(
-            [block[:, : cols // 2], block[:, cols // 2 :]], 0
+    def projection(turn, _):
+        @pl.when(turn == 1)
+        def _():
+            whole(1, o_all).wait_recv()
+            heads_f32[...] = o_all[slot_of(me, lax.rem(me + offset, N))].astype(jnp.float32)
+
+        mine = heads_f32[...]
+        n_out = steps * seqs
+        lhs = jnp.concatenate(
+            [mine[h * n_out : (h + 1) * n_out, :] for h in range(heads)], 1
         ).astype(jnp.bfloat16)
-        for o in ORDER:
-            send(2, sums, o, piece)
+
+        cols = w.shape[1] // PIECES
+        for piece in range(PIECES):
+            at = pl.ds(piece * cols, cols)
+            block = jnp.dot(lhs, w[:, at], preferred_element_type=jnp.float32)
+            sums[0, piece] = jnp.concatenate(
+                [block[:, : cols // 2], block[:, cols // 2 :]], 0
+            ).astype(jnp.bfloat16)
+
+            @pl.when(turn == 1)
+            def _():
+                for o in ORDER:
+                    send(2, sums, o, piece)
+
+        return 0
+
+    lax.fori_loop(0, 2, projection, 0)
     whole(2, sums).wait_recv()
     for phase, slots in enumerate((q_all, o_all, sums)):
         whole(phase, slots).wait_send()
@@ -250,7 +294,9 @@
         out_specs=(pl.BlockSpec(memory_space=pltpu.VMEM),) * 3,
         scratch_shapes=[
             pltpu.VMEM((steps, seqs, width), bf16),
-            pltpu.VMEM((2, seqs, ctx + PAD, 128), bf16),
+            pltpu.VMEM((ctx + PAD, seqs * 128), bf16),
+            pltpu.VMEM((ctx + PAD, seqs * 128), bf16),
+            pltpu.VMEM((seqs * 128, ctx + PAD), bf16),
             pltpu.VMEM((2, steps, seqs, 128), bf16),
             pltpu.SMEM((seqs,), jnp.int32),
             pltpu.SMEM((1,), jnp.int32),
@@ -259,6 +305,7 @@
             pltpu.VMEM((features,), bf16),
             pltpu.VMEM((heads * rows, 128), f32),
             pltpu.VMEM((2, rows, 128), f32),
+            pltpu.VMEM((heads * rows, 128), bf16),
             pltpu.VMEM((N, heads * rows, 128), bf16),
             pltpu.VMEM((N, heads * rows, 128), bf16),
             pltpu.SemaphoreType.DMA((10,)),

time: 26 us -> 25 us (0.962)
  Pallas kernels: 24.6 us -> 23.6 us
    pallas_call x1, Pallas kernels: 23.8 us -> 22.7 us  [shards(): pl.pallas_call(kernel, out_shape=(pltpu.VMEM((N, PIECES) + block, bf16),...]
where the time goes in v5:
time: 25 us; the launch traced here: 24.9 us
  Pallas kernels  23.6 us (94%)
  between operations  1.29 us (5%)
    pallas_call x1, Pallas kernels, shards(): pl.pallas_call(kernel, out_shape=(pltpu.VMEM((N, PIECES) + block, bf16),...  22.7 us
    pallas_call x1, Pallas kernels, shards(): pl.pallas_call(finish, out_shape=(out, out), in_specs=[pl.BlockSpec(memor...  0.83 us

profile of v5, /device:TPU:224, one launch (start us, length us, event | category | flops | bytes accessed | tf_op | source)
XLA Modules:
  0.0 24.9 jit_solution(4468081577732748036)
XLA Ops:
  1.3 22.7 %shard_map.95 = (bf16[8,4,16,512]{3,2,1,0:T(8,128)(2,1)S(1)}, f32[8,4096]{1,0:T(8,128)S(1)}, f32[8,4096]{1,0:T(8,128)S(1)}) custom-call(bf16[4,2,1024]{2,1,0:T(2,128)(2,1)} %q_hbm.1, bf16[2,2,4096,128]{3,2,1,0:T(8,128)(2,1)} %bitcast.2, bf16[2,4,2,128]{3,2,1,0:T(2,128)(2,1)} %bitcast.3, s32[2]{0:T(128)} %len_hbm.1, s32[1]{0:T(128)S(6)} %copy.10.spare_hbm, ...), custom_call_target="tpu_custom_call" | custom-call | tf_op jit(solution)/shard_map/pallas_call | solution.py:286
  24.0 0.8 %shard_map.96 = (bf16[4,2,4096]{2,1,0:T(2,128)(2,1)}, bf16[4,2,4096]{2,1,0:T(2,128)(2,1)}) custom-call(bf16[8,4,16,512]{3,2,1,0:T(8,128)(2,1)S(1)} %get-tuple-element.5.sums, f32[8,4096]{1,0:T(8,128)S(1)} %get-tuple-element.6.res, f32[8,4096]{1,0:T(8,128)S(1)} %get-tuple-element.7.gain), custom_call_target="tpu_custom_call" | custom-call | tf_op jit(solution)/shard_map/pallas_call | solution.py:321

commit v6 on v5

--- a/solution.py
+++ b/solution.py
@@ -201,34 +201,34 @@
         send(1, o_all, o)
     for copy in w_loads:
         copy.wait()
-    def projection(turn, _):
+    cols = w.shape[1] // PIECES
+    n_out = steps * seqs
+
+    def project(turn, _):
         @pl.when(turn == 1)
         def _():
             whole(1, o_all).wait_recv()
             heads_f32[...] = o_all[slot_of(me, lax.rem(me + offset, N))].astype(jnp.float32)
 
         mine = heads_f32[...]
-        n_out = steps * seqs
         lhs = jnp.concatenate(
             [mine[h * n_out : (h + 1) * n_out, :] for h in range(heads)], 1
         ).astype(jnp.bfloat16)
-
-        cols = w.shape[1] // PIECES
-        for piece in range(PIECES):
-            at = pl.ds(piece * cols, cols)
-            block = jnp.dot(lhs, w[:, at], preferred_element_type=jnp.float32)
-            sums[0, piece] = jnp.concatenate(
-                [block[:, : cols // 2], block[:, cols // 2 :]], 0
-            ).astype(jnp.bfloat16)
-
-            @pl.when(turn == 1)
-            def _():
-                for o in ORDER:
-                    send(2, sums, o, piece)
+        piece = lax.rem(turn + PIECES - 1, PIECES)
+        at = pl.ds(pl.multiple_of(piece * cols, cols), cols)
+        block = jnp.dot(lhs, w[:, at], preferred_element_type=jnp.float32)
+        sums[0, piece] = jnp.concatenate(
+            [block[:, : cols // 2], block[:, cols // 2 :]], 0
+        ).astype(jnp.bfloat16)
+
+        @pl.when(turn > 0)
+        def _():
+            for o in ORDER:
+                send(2, sums, o, piece)
 
         return 0
 
-    lax.fori_loop(0, 2, projection, 0)
+    lax.fori_loop(0, PIECES + 1, project, 0)
     whole(2, sums).wait_recv()
     for phase, slots in enumerate((q_all, o_all, sums)):
         whole(phase, slots).wait_send()

time: 25 us -> 25 us (level)
  no operation moved by 1% of the time
where the time goes in v6:
time: 25 us; the launch traced here: 24.9 us
  Pallas kernels  23.6 us (94%)
  between operations  1.29 us (5%)
    pallas_call x1, Pallas kernels, shards(): pl.pallas_call(kernel, out_shape=(pltpu.VMEM((N, PIECES) + block, bf16),...  22.8 us
    pallas_call x1, Pallas kernels, shards(): pl.pallas_call(finish, out_shape=(out, out), in_specs=[pl.BlockSpec(memor...  0.83 us

profile of v6, /device:TPU:224, one launch (start us, length us, event | category | flops | bytes accessed | tf_op | source)
XLA Modules:
  0.0 24.9 jit_solution(13055483540133470582)
XLA Ops:
  1.3 22.8 %shard_map.95 = (bf16[8,4,16,512]{3,2,1,0:T(8,128)(2,1)S(1)}, f32[8,4096]{1,0:T(8,128)S(1)}, f32[8,4096]{1,0:T(8,128)S(1)}) custom-call(bf16[4,2,1024]{2,1,0:T(2,128)(2,1)} %q_hbm.1, bf16[2,2,4096,128]{3,2,1,0:T(8,128)(2,1)} %bitcast.2, bf16[2,4,2,128]{3,2,1,0:T(2,128)(2,1)} %bitcast.3, s32[2]{0:T(128)} %len_hbm.1, s32[1]{0:T(128)S(6)} %copy.10.spare_hbm, ...), custom_call_target="tpu_custom_call" | custom-call | tf_op jit(solution)/shard_map/pallas_call | solution.py:286
  24.0 0.8 %shard_map.96 = (bf16[4,2,4096]{2,1,0:T(2,128)(2,1)}, bf16[4,2,4096]{2,1,0:T(2,128)(2,1)}) custom-call(bf16[8,4,16,512]{3,2,1,0:T(8,128)(2,1)S(1)} %get-tuple-element.5.sums, f32[8,4096]{1,0:T(8,128)S(1)} %get-tuple-element.6.res, f32[8,4096]{1,0:T(8,128)S(1)} %get-tuple-element.7.gain), custom_call_target="tpu_custom_call" | custom-call | tf_op jit(solution)/shard_map/pallas_call | solution.py:321

commit v7 on v6

--- a/solution.py
+++ b/solution.py
@@ -12,7 +12,8 @@
 PAD = 128
 WIDE = 4
 PIECES = 4
-ORDER = (6, 5, 7, 4, 2, 1, 3)
+ACROSS, ALONG_X = (6, 5, 7, 4), (2, 1, 3)
+ORDER = ACROSS + ALONG_X
 
 
 def partner(me, offset):
@@ -223,12 +224,14 @@
 
         @pl.when(turn > 0)
         def _():
-            for o in ORDER:
+            for o in ACROSS:
                 send(2, sums, o, piece)
 
         return 0
 
     lax.fori_loop(0, PIECES + 1, project, 0)
+    for o in ALONG_X:
+        send(2, sums, o)
     whole(2, sums).wait_recv()
     for phase, slots in enumerate((q_all, o_all, sums)):
         whole(phase, slots).wait_send()

time: 25 us -> 25.1 us (level)
  no operation moved by 1% of the time
where the time goes in v7:
time: 25.1 us; the launch traced here: 24.9 us
  Pallas kernels  23.6 us (94%)
  between operations  1.29 us (5%)
    pallas_call x1, Pallas kernels, shards(): pl.pallas_call(kernel, out_shape=(pltpu.VMEM((N, PIECES) + block, bf16),...  22.8 us
    pallas_call x1, Pallas kernels, shards(): pl.pallas_call(finish, out_shape=(out, out), in_specs=[pl.BlockSpec(memor...  0.83 us

profile of v7, /device:TPU:224, one launch (start us, length us, event | category | flops | bytes accessed | tf_op | source)
XLA Modules:
  0.0 24.9 jit_solution(9044125074872564636)
XLA Ops:
  1.3 22.8 %shard_map.95 = (bf16[8,4,16,512]{3,2,1,0:T(8,128)(2,1)S(1)}, f32[8,4096]{1,0:T(8,128)S(1)}, f32[8,4096]{1,0:T(8,128)S(1)}) custom-call(bf16[4,2,1024]{2,1,0:T(2,128)(2,1)} %q_hbm.1, bf16[2,2,4096,128]{3,2,1,0:T(8,128)(2,1)} %bitcast.2, bf16[2,4,2,128]{3,2,1,0:T(2,128)(2,1)} %bitcast.3, s32[2]{0:T(128)} %len_hbm.1, s32[1]{0:T(128)S(6)} %copy.10.spare_hbm, ...), custom_call_target="tpu_custom_call" | custom-call | tf_op jit(solution)/shard_map/pallas_call | solution.py:289
  24.1 0.8 %shard_map.96 = (bf16[4,2,4096]{2,1,0:T(2,128)(2,1)}, bf16[4,2,4096]{2,1,0:T(2,128)(2,1)}) custom-call(bf16[8,4,16,512]{3,2,1,0:T(8,128)(2,1)S(1)} %get-tuple-element.5.sums, f32[8,4096]{1,0:T(8,128)S(1)} %get-tuple-element.6.res, f32[8,4096]{1,0:T(8,128)S(1)} %get-tuple-element.7.gain), custom_call_target="tpu_custom_call" | custom-call | tf_op jit(solution)/shard_map/pallas_call | solution.py:324
